TPU v7x, 32 devices: a whole 2x2x4 slice. The times are simulated.
32 devices in a mesh: gx: 8 (over z, core), gy: 4 (over y, x).
Axes of the slice: x: 2, y: 2, z: 4, core: 2. Of those that a mesh axis runs over, the one named last changes fastest.
Arguments:
- coil_sources: float32 [8, 128, 128, 128], P(None, 'gx', 'gy'), may hold values from -6 to 6
- tissue_labels: int32 [128, 128, 128], P('gx', 'gy'), may hold values from 0 to 5
- class_conductivity: float32 [6], replicated, may hold values from 0.1 to 2
Outputs:
- potential: float32 [8, 128, 128, 128], P(None, 'gx', 'gy')
All inputs are finite; a program needn't handle non-finite values.
Results may differ from a plain program's by a relative error of at most 0.0003.
Values sent between devices are 32-bit elements; how exact they have to be, the bound alone decides.
A program may use at most 192 MiB of HBM per device.

v0:
```python
import jax
import jax.numpy as jnp
from jax import lax
from jax.sharding import PartitionSpec as P

LEVELS = 5
SWEEPS = 2
COARSE_SWEEPS = 16
CLASSES = 6
damping = 0.8


def padded(cells, sides, width):
    for axis, dim in sides:
        count = lax.axis_size(axis)
        ends = count - 1
        head = lax.slice_in_dim(cells, 0, width, axis=dim)
        tail = lax.slice_in_dim(cells, cells.shape[dim] - width, cells.shape[dim], axis=dim)
        cells = jnp.concatenate(
            [
                lax.ppermute(tail, axis, [(i, (i + 1) % count) for i in range(ends)]),
                cells,
                lax.ppermute(head, axis, [((i + 1) % count, i) for i in range(ends)]),
            ],
            axis=dim,
        )
    return cells


def lookup_table(labels, table):
    result = jnp.zeros(labels.shape, jnp.float32)
    for klass in range(CLASSES):
        result = result + jnp.where(labels == klass, table[klass], jnp.float32(0.0))
    return result


def coarsen_cond(cond):
    sx, sy, sz = cond.shape
    return cond.reshape(sx // 2, 2, sy // 2, 2, sz // 2, 2).mean(axis=(1, 3, 5))


def restrict_sum(field):
    rr, sx, sy, sz = field.shape
    return field.reshape(rr, sx // 2, 2, sy // 2, 2, sz // 2, 2).sum(axis=(2, 4, 6))


def prolong_copy(field):
    rr, sx, sy, sz = field.shape
    grown = jnp.broadcast_to(field[:, :, None, :, None, :, None], (rr, sx, 2, sy, 2, sz, 2))
    return grown.reshape(rr, 2 * sx, 2 * sy, 2 * sz)


def face_coeffs(extended):
    centre = extended[1:-1, 1:-1, :]
    zpadded = jnp.pad(centre, ((0, 0), (0, 0), (1, 1)))
    others = [
        extended[2:, 1:-1, :],
        extended[:-2, 1:-1, :],
        extended[1:-1, 2:, :],
        extended[1:-1, :-2, :],
        zpadded[:, :, 2:],
        zpadded[:, :, :-2],
    ]
    coeffs = [
        jnp.where(other > 0, 2.0 * centre * other / (centre + other), centre) for other in others
    ]
    face_sum = coeffs[0] + coeffs[1] + coeffs[2] + coeffs[3] + coeffs[4] + coeffs[5]
    return (coeffs, face_sum)


def apply_operator(extended, field, coeffs, face_sum, scale):
    zpadded = jnp.pad(field, ((0, 0), (0, 0), (0, 0), (1, 1)))
    others = [
        extended[:, 2:, 1:-1, :],
        extended[:, :-2, 1:-1, :],
        extended[:, 1:-1, 2:, :],
        extended[:, 1:-1, :-2, :],
        zpadded[:, :, :, 2:],
        zpadded[:, :, :, :-2],
    ]
    total = coeffs[0] * others[0]
    for index in range(1, 6):
        total = total + coeffs[index] * others[index]
    return scale * (face_sum * field - total)


def field_rim(field):
    return padded(field, (("gx", 1), ("gy", 2)), 1)


def cond_rim(cond):
    return padded(cond, (("gx", 0), ("gy", 1)), 1)


def local_field_pad(field):
    return jnp.pad(field, ((0, 0), (1, 1), (1, 1), (0, 0)))


def local_cond_pad(cond):
    return jnp.pad(cond, ((1, 1), (1, 1), (0, 0)))


def relax(field, source, coeffs, face_sum, scale, count, padder):
    diagonal = scale * face_sum
    for sweep_index in range(count):
        field = (
            field
            + damping
            * (source - apply_operator(padder(field), field, coeffs, face_sum, scale))
            / diagonal
        )
    return field


def local_vcycle(level, source, conductivities, first):
    scale = jnp.float32(2.0**level)
    coeffs, face_sum = face_coeffs(local_cond_pad(conductivities[level - first]))
    diagonal = scale * face_sum
    field = damping * source / diagonal
    return relax(field, source, coeffs, face_sum, scale, COARSE_SWEEPS - 1, local_field_pad)


def local(coil_sources, tissue_labels, class_conductivity):
    depth = LEVELS - 1
    conductivities = [lookup_table(tissue_labels, class_conductivity)]
    for level in range(depth):
        conductivities.append(coarsen_cond(conductivities[-1]))
    stored = []
    source = coil_sources
    for level in range(depth):
        scale = jnp.float32(2.0**level)
        coeffs, face_sum = face_coeffs(cond_rim(conductivities[level]))
        field = damping * source / (scale * face_sum)
        field = relax(field, source, coeffs, face_sum, scale, SWEEPS - 1, field_rim)
        residual = source - apply_operator(field_rim(field), field, coeffs, face_sum, scale)
        stored.append((field, source, coeffs, face_sum, source, scale))
        source = restrict_sum(residual)
    block_x = source.shape[1]
    block_y = source.shape[2]
    gathered, coarse_cond = (
        lax.all_gather(source, "gy", axis=2, tiled=True),
        lax.all_gather(conductivities[depth], "gy", axis=1, tiled=True),
    )
    gathered, coarse_cond = (
        lax.all_gather(gathered, "gx", axis=1, tiled=True),
        lax.all_gather(coarse_cond, "gx", axis=0, tiled=True),
    )
    coarse_list = [coarse_cond]
    correction = local_vcycle(depth, gathered, coarse_list, depth)
    correction = lax.dynamic_slice_in_dim(correction, lax.axis_index("gx") * block_x, block_x, 1)
    correction = lax.dynamic_slice_in_dim(correction, lax.axis_index("gy") * block_y, block_y, 2)
    for level in range(depth - 1, -1, -1):
        field, source, coeffs, face_sum, source_ext, scale = stored[level]
        field = field + prolong_copy(correction)
        correction = relax(field, source, coeffs, face_sum, scale, SWEEPS, field_rim)
    return correction


def solution(mesh):
    in_specs = (P(None, "gx", "gy", None), P("gx", "gy", None), P())
    out_specs = P(None, "gx", "gy", None)
    return jax.shard_map(local, mesh=mesh, in_specs=in_specs, out_specs=out_specs, check_vma=False)
```

profile of v0, /device:TPU:16, one launch (start us, length us, event | category | flops | bytes accessed | tf_op | source)
XLA Modules:
  0.0 563.2 jit_solution(10171521428862776019)
XLA Ops:
  1.5 5.0 select_add_fusion
  8.5 3.6 collective-permute-start
  12.1 18.1 %reshape.94 = f32[8,2,16,2,64,2]{5,4,3,2,1,0:T(8,128)} reshape(f32[16,32,128]{2,1,0:T(8,128)S(1)} %select_add_fusion) | data formatting | bytes 524288 | tf_op jit(solution)/shard_map/reshape | solution.py:39
  30.2 7.0 %reduce_sum.89 = f32[8,16,64]{2,1,0:T(8,128)S(1)} reduce(f32[8,2,16,2,64,2]{5,4,3,2,1,0:T(8,128)} %reshape.94, f32[]{:T(128)} %constant.32.clone.1), dimensions={1,3,5}, to_apply=%region_1.2 | reduce | flops 57344 | bytes 294916 | tf_op jit(solution)/shard_map/reduce_sum | solution.py:39
  39.8 3.6 collective-permute-start.12
  43.5 3.5 div.336
  50.3 4.5 collective-permute-start.3
  56.2 3.2 add_add_fusion
  66.7 3.1 collective-permute-start.25
  76.4 4.3 collective-permute-start.7
  83.4 6.3 %collective-permute-start.15 = (f32[10,1,64]{2,1,0:T(1,128)S(1)}, f32[10,1,64]{2,1,0:T(1,128)S(1)}, u32[]{:S(2)}, u32[]{:S(2)}) collective-permute-start(f32[10,1,64]{2,1,0:T(1,128)S(1)} %get-tuple-element.103), channel_id=1, source_target_pairs={{0,1},{1,2},{2,3},{4,5},{5,6},{6,7},{8,9},{9,10},{10,11},{12,13},{... | collective-permute-start | bytes 7688 | tf_op jit(solution)/shard_map/ppermute | solution.py:21
  90.0 4.6 fusion.7
  103.0 4.8 collective-permute-start.11
  110.4 3.7 collective-permute-done.10
  114.2 4.4 fusion.13
  118.6 18.0 %copy.522 = f32[8,16,32,128]{0,3,2,1:T(8,128)} copy(f32[8,16,32,128]{3,2,1,0:T(8,128)} %fusion.13) | data formatting | bytes 4194304 | tf_op jit(solution)/shard_map/sub | solution.py:135
  136.6 24.3 %reduce_sum.88 = f32[8,8,16,64]{0,3,2,1:T(8,128)} reduce(f32[8,8,2,16,2,64,2]{0,6,5,4,3,2,1:T(2,128)} %bitcast.21, f32[]{:T(128)} %constant.32.clone.1), dimensions={2,4,6}, to_apply=%region_0.1 | reduce | flops 458752 | bytes 2359300 | tf_op jit(solution)/shard_map/reduce_sum | solution.py:44
  160.8 2.9 copy.523
  172.4 4.8 collective-permute-start.19
  180.6 5.2 collective-permute-start.27
  194.1 4.8 collective-permute-start.23
  200.9 3.9 collective-permute-done.22
  208.1 4.8 reduce_sum.90
  219.8 3.7 collective-permute-start.37
  231.9 5.2 collective-permute-start.39
  237.1 3.1 fusion.69
  249.2 5.4 collective-permute-start.35
  261.8 3.8 fusion.76
  274.1 7.1 %all-gather.4 = f32[4,2,8]{2,1,0:T(2,128)S(1)} all-gather(f32[1,2,8]{2,1,0:T(2,128)} %multiply_bitcast_fusion), channel_id=4, replica_groups=mesh['gx'=8,'gy'=4] {'gy'}, dimensions={0}, use_global_device_ids=true | all-gather | bytes 320 | tf_op jit(solution)/shard_map/all_gather | solution.py:142
  281.2 13.3 %all-gather.3 = f32[64,8]{1,0:T(8,128)S(1)} all-gather(f32[8,8]{1,0:T(8,128)S(1)} %bitcast.46), channel_id=5, replica_groups=mesh['gx'=8,'gy'=4] {'gx'}, dimensions={0}, use_global_device_ids=true | all-gather | bytes 2304 | tf_op jit(solution)/shard_map/all_gather | solution.py:146
  295.2 3.3 collective-permute-start.43
  300.5 3.8 collective-permute-done.42
  305.7 3.2 collective-permute-start.44
  310.8 3.3 collective-permute-done.45
  314.1 4.3 collective-permute-start.47
  320.3 3.9 collective-permute-done.46
  328.6 7.7 %all-gather = f32[8,8,8]{2,0,1:T(8,128)S(1)} all-gather(f32[8,2,8]{2,0,1:T(8,128)} %copy.527), channel_id=2, replica_groups=mesh['gx'=8,'gy'=4] {'gy'}, dimensions={1}, use_global_device_ids=true | all-gather | bytes 2560 | tf_op jit(solution)/shard_map/all_gather | solution.py:141
  336.3 13.0 %all-gather.1 = f32[8,64,8]{2,0,1:T(8,128)S(1)} all-gather(f32[8,8,8]{2,0,1:T(8,128)S(1)} %all-gather), channel_id=3, replica_groups=mesh['gx'=8,'gy'=4] {'gx'}, dimensions={1}, use_global_device_ids=true | all-gather | bytes 18432 | tf_op jit(solution)/shard_map/all_gather | solution.py:145
  356.4 4.6 collective-permute-start.48
  362.9 3.3 collective-permute-done.49
  366.2 3.0 collective-permute-start.51
  370.8 4.2 collective-permute-done.50
  383.5 4.3 collective-permute-start.55
  389.4 4.2 collective-permute-done.54
  399.5 3.8 collective-permute-done.57
  403.3 2.8 collective-permute-start.59
  408.3 4.3 collective-permute-done.58
  418.7 3.8 collective-permute-done.61
  427.5 4.3 collective-permute-done.62
  433.4 4.2 broadcast_in_dim.54
  437.5 3.6 copy.529
  446.8 3.2 collective-permute-done.65
  454.5 4.2 collective-permute-done.66
  463.8 3.2 collective-permute-done.69
  471.6 4.2 collective-permute-done.70
  477.2 3.6 copy.532
  480.8 16.0 %broadcast_in_dim.55 = f32[8,8,2,16,2,64,2]{0,6,5,4,3,2,1:T(2,128)} broadcast(f32[8,8,16,64]{0,3,2,1:T(8,128)} %copy.532), dimensions={0,1,3,5} | broadcast | bytes 2359296 | tf_op jit(solution)/shard_map/broadcast_in_dim | solution.py:49
  496.8 20.1 %copy.533 = f32[8,16,32,128]{3,2,1,0:T(8,128)} copy(f32[8,16,32,128]{0,3,2,1:T(8,128)} %bitcast.22) | data formatting | bytes 4194304 | tf_op jit(solution)/shard_map/reshape | solution.py:50
  524.2 3.8 collective-permute-done.73
  533.0 4.2 collective-permute-done.74
  537.4 3.6 fusion.22
  545.4 3.8 collective-permute-done.77
  554.2 4.2 collective-permute-done.78
  558.5 4.5 fusion.31
  (419 shorter events, 198.9 us)
Async XLA Ops:
  6.5 42.4 %collective-permute-start.1 = (f32[1,32,128]{2,1,0:T(8,128)S(1)}, f32[1,32,128]{2,1,0:T(8,128)S(1)}, u32[]{:S(2)}, u32[]{:S(2)}) collective-permute-start(f32[1,32,128]{2,1,0:T(8,128)S(1)} %get-tuple-element.94), channel_id=1, source_target_pairs={{0,4},{4,8},{8,12},{12,16},{16,20},{20,24},{24,28},{1,5},{5,9},{9,... | collective-permute-start | bytes 49160 | tf_op jit(solution)/shard_map/ppermute | solution.py:21
  8.5 40.5 %collective-permute-start = (f32[1,32,128]{2,1,0:T(8,128)S(1)}, f32[1,32,128]{2,1,0:T(8,128)S(1)}, u32[]{:S(2)}, u32[]{:S(2)}) collective-permute-start(f32[1,32,128]{2,1,0:T(8,128)S(1)} %get-tuple-element.93), channel_id=1, source_target_pairs={{4,0},{8,4},{12,8},{16,12},{20,16},{24,20},{28,24},{5,1},{9,5},{13... | collective-permute-start | bytes 49160 | tf_op jit(solution)/shard_map/ppermute | solution.py:23
  37.9 42.8 %collective-permute-start.13 = (f32[1,16,64]{2,1,0:T(8,128)}, f32[1,16,64]{2,1,0:T(8,128)S(1)}, u32[]{:S(2)}, u32[]{:S(2)}) collective-permute-start(f32[1,16,64]{2,1,0:T(8,128)} %get-tuple-element.114), channel_id=1, source_target_pairs={{0,4},{4,8},{8,12},{12,16},{16,20},{20,24},{24,28},{1,5},{5,9},{9,... | collective-permute-start | bytes 12296 | tf_op jit(solution)/shard_map/ppermute | solution.py:21
  39.8 42.2 %collective-permute-start.12 = (f32[1,16,64]{2,1,0:T(8,128)}, f32[1,16,64]{2,1,0:T(8,128)S(1)}, u32[]{:S(2)}, u32[]{:S(2)}) collective-permute-start(f32[1,16,64]{2,1,0:T(8,128)} %get-tuple-element.113), channel_id=1, source_target_pairs={{4,0},{8,4},{12,8},{16,12},{20,16},{24,20},{28,24},{5,1},{9,5},{13... | collective-permute-start | bytes 12296 | tf_op jit(solution)/shard_map/ppermute | solution.py:23
  49.0 5.9 %collective-permute-start.2 = (f32[18,1,128]{2,1,0:T(1,128)S(1)}, f32[18,1,128]{2,1,0:T(1,128)S(1)}, u32[]{:S(2)}, u32[]{:S(2)}) collective-permute-start(f32[18,1,128]{2,1,0:T(1,128)S(1)} %get-tuple-element.92), channel_id=1, source_target_pairs={{1,0},{2,1},{3,2},{5,4},{6,5},{7,6},{9,8},{10,9},{11,10},{13,12},{... | collective-permute-start | bytes 27656 | tf_op jit(solution)/shard_map/ppermute | solution.py:23
  50.3 5.9 %collective-permute-start.3 = (f32[18,1,128]{2,1,0:T(1,128)S(1)}, f32[18,1,128]{2,1,0:T(1,128)S(1)}, u32[]{:S(2)}, u32[]{:S(2)}) collective-permute-start(f32[18,1,128]{2,1,0:T(1,128)S(1)} %get-tuple-element.91), channel_id=1, source_target_pairs={{0,1},{1,2},{2,3},{4,5},{5,6},{6,7},{8,9},{9,10},{10,11},{12,13},{... | collective-permute-start | bytes 27656 | tf_op jit(solution)/shard_map/ppermute | solution.py:21
  61.8 10.6 %collective-permute-start.4 = (f32[8,1,32,128]{3,2,1,0:T(8,128)}, f32[8,1,32,128]{3,2,1,0:T(8,128)}, u32[]{:S(2)}, u32[]{:S(2)}) collective-permute-start(f32[8,1,32,128]{3,2,1,0:T(8,128)} %get-tuple-element.58), channel_id=1, source_target_pairs={{4,0},{8,4},{12,8},{16,12},{20,16},{24,20},{28,24},{5,1},{9,5},{13... | collective-permute-start | bytes 393224 | tf_op jit(solution)/shard_map/ppermute | solution.py:23
  63.7 11.3 %collective-permute-start.5 = (f32[8,1,32,128]{3,2,1,0:T(8,128)}, f32[8,1,32,128]{3,2,1,0:T(8,128)}, u32[]{:S(2)}, u32[]{:S(2)}) collective-permute-start(f32[8,1,32,128]{3,2,1,0:T(8,128)} %get-tuple-element.57), channel_id=1, source_target_pairs={{0,4},{4,8},{8,12},{12,16},{16,20},{20,24},{24,28},{1,5},{5,9},{9,... | collective-permute-start | bytes 393224 | tf_op jit(solution)/shard_map/ppermute | solution.py:21
  66.7 111.8 %collective-permute-start.25 = (f32[1,8,32]{2,1,0:T(8,128)}, f32[1,8,32]{2,1,0:T(8,128)}, u32[]{:S(2)}, u32[]{:S(2)}) collective-permute-start(f32[1,8,32]{2,1,0:T(8,128)} %get-tuple-element.118), channel_id=1, source_target_pairs={{0,4},{4,8},{8,12},{12,16},{16,20},{20,24},{24,28},{1,5},{5,9},{9,... | collective-permute-start | bytes 3080 | tf_op jit(solution)/shard_map/ppermute | solution.py:21
  72.4 106.1 %collective-permute-start.24 = (f32[1,8,32]{2,1,0:T(8,128)}, f32[1,8,32]{2,1,0:T(8,128)}, u32[]{:S(2)}, u32[]{:S(2)}) collective-permute-start(f32[1,8,32]{2,1,0:T(8,128)} %get-tuple-element.117), channel_id=1, source_target_pairs={{4,0},{8,4},{12,8},{16,12},{20,16},{24,20},{28,24},{5,1},{9,5},{13... | collective-permute-start | bytes 3080 | tf_op jit(solution)/shard_map/ppermute | solution.py:23
  76.4 7.0 %collective-permute-start.7 = (f32[8,18,1,128]{3,0,2,1:T(8,128)S(1)}, f32[8,18,1,128]{3,0,2,1:T(8,128)S(1)}, u32[]{:S(2)}, u32[]{:S(2)}) collective-permute-start(f32[8,18,1,128]{3,0,2,1:T(8,128)S(1)} %copy.516), channel_id=1, source_target_pairs={{0,1},{1,2},{2,3},{4,5},{5,6},{6,7},{8,9},{9,10},{10,11},{12,13},{... | collective-permute-start | bytes 221192 | tf_op jit(solution)/shard_map/ppermute | solution.py:21
  80.7 9.1 %collective-permute-start.6 = (f32[8,18,1,128]{3,0,2,1:T(8,128)S(1)}, f32[8,18,1,128]{3,0,2,1:T(8,128)S(1)}, u32[]{:S(2)}, u32[]{:S(2)}) collective-permute-start(f32[8,18,1,128]{3,0,2,1:T(8,128)S(1)} %copy.514), channel_id=1, source_target_pairs={{1,0},{2,1},{3,2},{5,4},{6,5},{7,6},{9,8},{10,9},{11,10},{13,12},{... | collective-permute-start | bytes 221192 | tf_op jit(solution)/shard_map/ppermute | solution.py:23
  82.1 14.5 %collective-permute-start.14 = (f32[10,1,64]{2,1,0:T(1,128)S(1)}, f32[10,1,64]{2,1,0:T(1,128)S(1)}, u32[]{:S(2)}, u32[]{:S(2)}) collective-permute-start(f32[10,1,64]{2,1,0:T(1,128)S(1)} %get-tuple-element.104), channel_id=1, source_target_pairs={{1,0},{2,1},{3,2},{5,4},{6,5},{7,6},{9,8},{10,9},{11,10},{13,12},{... | collective-permute-start | bytes 7688 | tf_op jit(solution)/shard_map/ppermute | solution.py:23
  83.4 15.6 %collective-permute-start.15 = (f32[10,1,64]{2,1,0:T(1,128)S(1)}, f32[10,1,64]{2,1,0:T(1,128)S(1)}, u32[]{:S(2)}, u32[]{:S(2)}) collective-permute-start(f32[10,1,64]{2,1,0:T(1,128)S(1)} %get-tuple-element.103), channel_id=1, source_target_pairs={{0,1},{1,2},{2,3},{4,5},{5,6},{6,7},{8,9},{9,10},{10,11},{12,13},{... | collective-permute-start | bytes 7688 | tf_op jit(solution)/shard_map/ppermute | solution.py:21
  94.6 5.9 %collective-permute-start.8 = (f32[8,1,32,128]{3,2,1,0:T(8,128)S(1)}, f32[8,1,32,128]{3,2,1,0:T(8,128)S(1)}, u32[]{:S(2)}, u32[]{:S(2)}) collective-permute-start(f32[8,1,32,128]{3,2,1,0:T(8,128)S(1)} %get-tuple-element.56), channel_id=1, source_target_pairs={{4,0},{8,4},{12,8},{16,12},{20,16},{24,20},{28,24},{5,1},{9,5},{13... | collective-permute-start | bytes 393224 | tf_op jit(solution)/shard_map/ppermute | solution.py:23
  96.6 6.3 %collective-permute-start.9 = (f32[8,1,32,128]{3,2,1,0:T(8,128)S(1)}, f32[8,1,32,128]{3,2,1,0:T(8,128)S(1)}, u32[]{:S(2)}, u32[]{:S(2)}) collective-permute-start(f32[8,1,32,128]{3,2,1,0:T(8,128)S(1)} %get-tuple-element.55), channel_id=1, source_target_pairs={{0,4},{4,8},{8,12},{12,16},{16,20},{20,24},{24,28},{1,5},{5,9},{9,... | collective-permute-start | bytes 393224 | tf_op jit(solution)/shard_map/ppermute | solution.py:21
  103.0 7.3 %collective-permute-start.11 = (f32[8,18,1,128]{3,0,2,1:T(8,128)S(1)}, f32[8,18,1,128]{3,0,2,1:T(8,128)S(1)}, u32[]{:S(2)}, u32[]{:S(2)}) collective-permute-start(f32[8,18,1,128]{3,0,2,1:T(8,128)S(1)} %copy.520), channel_id=1, source_target_pairs={{0,1},{1,2},{2,3},{4,5},{5,6},{6,7},{8,9},{9,10},{10,11},{12,13},{... | collective-permute-start | bytes 221192 | tf_op jit(solution)/shard_map/ppermute | solution.py:21
  107.8 6.2 %collective-permute-start.10 = (f32[8,18,1,128]{3,0,2,1:T(8,128)S(1)}, f32[8,18,1,128]{3,0,2,1:T(8,128)S(1)}, u32[]{:S(2)}, u32[]{:S(2)}) collective-permute-start(f32[8,18,1,128]{3,0,2,1:T(8,128)S(1)} %copy.518), channel_id=1, source_target_pairs={{1,0},{2,1},{3,2},{5,4},{6,5},{7,6},{9,8},{10,9},{11,10},{13,12},{... | collective-permute-start | bytes 221192 | tf_op jit(solution)/shard_map/ppermute | solution.py:23
  164.8 5.6 collective-permute-start.16
  166.7 5.6 collective-permute-start.17
  172.4 13.4 %collective-permute-start.19 = (f32[8,10,1,64]{3,2,1,0:T(1,128)S(1)}, f32[8,10,1,64]{3,2,1,0:T(1,128)S(1)}, u32[]{:S(2)}, u32[]{:S(2)}) collective-permute-start(f32[8,10,1,64]{3,2,1,0:T(1,128)S(1)} %get-tuple-element.74), channel_id=1, source_target_pairs={{0,1},{1,2},{2,3},{4,5},{5,6},{6,7},{8,9},{9,10},{10,11},{12,13},{... | collective-permute-start | bytes 61448 | tf_op jit(solution)/shard_map/ppermute | solution.py:21
  177.2 8.6 %collective-permute-start.18 = (f32[8,10,1,64]{3,2,1,0:T(1,128)S(1)}, f32[8,10,1,64]{3,2,1,0:T(1,128)S(1)}, u32[]{:S(2)}, u32[]{:S(2)}) collective-permute-start(f32[8,10,1,64]{3,2,1,0:T(1,128)S(1)} %get-tuple-element.73), channel_id=1, source_target_pairs={{1,0},{2,1},{3,2},{5,4},{6,5},{7,6},{9,8},{10,9},{11,10},{13,12},{... | collective-permute-start | bytes 61448 | tf_op jit(solution)/shard_map/ppermute | solution.py:23
  179.3 11.6 %collective-permute-start.26 = (f32[6,1,32]{2,1,0:T(1,128)S(1)}, f32[6,1,32]{2,1,0:T(1,128)S(1)}, u32[]{:S(2)}, u32[]{:S(2)}) collective-permute-start(f32[6,1,32]{2,1,0:T(1,128)S(1)} %get-tuple-element.116), channel_id=1, source_target_pairs={{1,0},{2,1},{3,2},{5,4},{6,5},{7,6},{9,8},{10,9},{11,10},{13,12},{... | collective-permute-start | bytes 2312 | tf_op jit(solution)/shard_map/ppermute | solution.py:23
  180.6 10.3 %collective-permute-start.27 = (f32[6,1,32]{2,1,0:T(1,128)S(1)}, f32[6,1,32]{2,1,0:T(1,128)S(1)}, u32[]{:S(2)}, u32[]{:S(2)}) collective-permute-start(f32[6,1,32]{2,1,0:T(1,128)S(1)} %get-tuple-element.115), channel_id=1, source_target_pairs={{0,1},{1,2},{2,3},{4,5},{5,6},{6,7},{8,9},{9,10},{10,11},{12,13},{... | collective-permute-start | bytes 2312 | tf_op jit(solution)/shard_map/ppermute | solution.py:21
  186.5 5.8 %collective-permute-start.20 = (f32[8,1,16,64]{3,2,1,0:T(8,128)S(1)}, f32[8,1,16,64]{3,2,1,0:T(8,128)S(1)}, u32[]{:S(2)}, u32[]{:S(2)}) collective-permute-start(f32[8,1,16,64]{3,2,1,0:T(8,128)S(1)} %get-tuple-element.88), channel_id=1, source_target_pairs={{4,0},{8,4},{12,8},{16,12},{20,16},{24,20},{28,24},{5,1},{9,5},{13... | collective-permute-start | bytes 98312 | tf_op jit(solution)/shard_map/ppermute | solution.py:23
  188.4 5.6 collective-permute-start.21
  194.1 6.7 %collective-permute-start.23 = (f32[8,10,1,64]{3,2,1,0:T(1,128)S(1)}, f32[8,10,1,64]{3,2,1,0:T(1,128)S(1)}, u32[]{:S(2)}, u32[]{:S(2)}) collective-permute-start(f32[8,10,1,64]{3,2,1,0:T(1,128)S(1)} %get-tuple-element.72), channel_id=1, source_target_pairs={{0,1},{1,2},{2,3},{4,5},{5,6},{6,7},{8,9},{9,10},{10,11},{12,13},{... | collective-permute-start | bytes 61448 | tf_op jit(solution)/shard_map/ppermute | solution.py:21
  198.9 5.9 %collective-permute-start.22 = (f32[8,10,1,64]{3,2,1,0:T(1,128)S(1)}, f32[8,10,1,64]{3,2,1,0:T(1,128)S(1)}, u32[]{:S(2)}, u32[]{:S(2)}) collective-permute-start(f32[8,10,1,64]{3,2,1,0:T(1,128)S(1)} %get-tuple-element.71), channel_id=1, source_target_pairs={{1,0},{2,1},{3,2},{5,4},{6,5},{7,6},{9,8},{10,9},{11,10},{13,12},{... | collective-permute-start | bytes 61448 | tf_op jit(solution)/shard_map/ppermute | solution.py:23
  214.8 10.6 %collective-permute-start.28 = (f32[8,1,8,32]{0,3,2,1:T(8,128)}, f32[8,1,8,32]{0,3,2,1:T(8,128)}, u32[]{:S(2)}, u32[]{:S(2)}) collective-permute-start(f32[8,1,8,32]{0,3,2,1:T(8,128)} %get-tuple-element.86), channel_id=1, source_target_pairs={{4,0},{8,4},{12,8},{16,12},{20,16},{24,20},{28,24},{5,1},{9,5},{13... | collective-permute-start | bytes 24584 | tf_op jit(solution)/shard_map/ppermute | solution.py:23
  216.7 8.7 %collective-permute-start.29 = (f32[8,1,8,32]{0,3,2,1:T(8,128)}, f32[8,1,8,32]{0,3,2,1:T(8,128)}, u32[]{:S(2)}, u32[]{:S(2)}) collective-permute-start(f32[8,1,8,32]{0,3,2,1:T(8,128)} %get-tuple-element.85), channel_id=1, source_target_pairs={{0,4},{4,8},{8,12},{12,16},{16,20},{20,24},{24,28},{1,5},{5,9},{9,... | collective-permute-start | bytes 24584 | tf_op jit(solution)/shard_map/ppermute | solution.py:21
  219.8 10.8 %collective-permute-start.37 = (f32[1,4,16]{2,1,0:T(4,128)}, f32[1,4,16]{2,1,0:T(4,128)S(1)}, u32[]{:S(2)}, u32[]{:S(2)}) collective-permute-start(f32[1,4,16]{2,1,0:T(4,128)} %get-tuple-element.123), channel_id=1, source_target_pairs={{0,4},{4,8},{8,12},{12,16},{16,20},{20,24},{24,28},{1,5},{5,9},{9,... | collective-permute-start | bytes 776 | tf_op jit(solution)/shard_map/ppermute | solution.py:21
  223.5 7.0 %collective-permute-start.36 = (f32[1,4,16]{2,1,0:T(4,128)}, f32[1,4,16]{2,1,0:T(4,128)S(1)}, u32[]{:S(2)}, u32[]{:S(2)}) collective-permute-start(f32[1,4,16]{2,1,0:T(4,128)} %get-tuple-element.122), channel_id=1, source_target_pairs={{4,0},{8,4},{12,8},{16,12},{20,16},{24,20},{28,24},{5,1},{9,5},{13... | collective-permute-start | bytes 776 | tf_op jit(solution)/shard_map/ppermute | solution.py:23
  226.4 10.7 %collective-permute-start.31 = (f32[8,6,1,32]{0,3,2,1:T(8,128)S(1)}, f32[8,6,1,32]{0,3,2,1:T(8,128)S(1)}, u32[]{:S(2)}, u32[]{:S(2)}) collective-permute-start(f32[8,6,1,32]{0,3,2,1:T(8,128)S(1)} %get-tuple-element.66), channel_id=1, source_target_pairs={{0,1},{1,2},{2,3},{4,5},{5,6},{6,7},{8,9},{9,10},{10,11},{12,13},{... | collective-permute-start | bytes 18440 | tf_op jit(solution)/shard_map/ppermute | solution.py:21
  229.2 7.9 %collective-permute-start.30 = (f32[8,6,1,32]{0,3,2,1:T(8,128)S(1)}, f32[8,6,1,32]{0,3,2,1:T(8,128)S(1)}, u32[]{:S(2)}, u32[]{:S(2)}) collective-permute-start(f32[8,6,1,32]{0,3,2,1:T(8,128)S(1)} %get-tuple-element.65), channel_id=1, source_target_pairs={{1,0},{2,1},{3,2},{5,4},{6,5},{7,6},{9,8},{10,9},{11,10},{13,12},{... | collective-permute-start | bytes 18440 | tf_op jit(solution)/shard_map/ppermute | solution.py:23
  230.6 14.0 %collective-permute-start.38 = (f32[4,1,16]{2,1,0:T(1,128)S(1)}, f32[4,1,16]{2,1,0:T(1,128)S(1)}, u32[]{:S(2)}, u32[]{:S(2)}) collective-permute-start(f32[4,1,16]{2,1,0:T(1,128)S(1)} %get-tuple-element.120), channel_id=1, source_target_pairs={{1,0},{2,1},{3,2},{5,4},{6,5},{7,6},{9,8},{10,9},{11,10},{13,12},{... | collective-permute-start | bytes 776 | tf_op jit(solution)/shard_map/ppermute | solution.py:23
  231.9 12.7 %collective-permute-start.39 = (f32[4,1,16]{2,1,0:T(1,128)S(1)}, f32[4,1,16]{2,1,0:T(1,128)S(1)}, u32[]{:S(2)}, u32[]{:S(2)}) collective-permute-start(f32[4,1,16]{2,1,0:T(1,128)S(1)} %get-tuple-element.119), channel_id=1, source_target_pairs={{0,1},{1,2},{2,3},{4,5},{5,6},{6,7},{8,9},{9,10},{10,11},{12,13},{... | collective-permute-start | bytes 776 | tf_op jit(solution)/shard_map/ppermute | solution.py:21
  240.2 6.4 %collective-permute-start.32 = (f32[8,1,8,32]{0,3,2,1:T(8,128)S(1)}, f32[8,1,8,32]{0,3,2,1:T(8,128)S(1)}, u32[]{:S(2)}, u32[]{:S(2)}) collective-permute-start(f32[8,1,8,32]{0,3,2,1:T(8,128)S(1)} %get-tuple-element.84), channel_id=1, source_target_pairs={{4,0},{8,4},{12,8},{16,12},{20,16},{24,20},{28,24},{5,1},{9,5},{13... | collective-permute-start | bytes 24584 | tf_op jit(solution)/shard_map/ppermute | solution.py:23
  242.2 6.3 %collective-permute-start.33 = (f32[8,1,8,32]{0,3,2,1:T(8,128)S(1)}, f32[8,1,8,32]{0,3,2,1:T(8,128)S(1)}, u32[]{:S(2)}, u32[]{:S(2)}) collective-permute-start(f32[8,1,8,32]{0,3,2,1:T(8,128)S(1)} %get-tuple-element.83), channel_id=1, source_target_pairs={{0,4},{4,8},{8,12},{12,16},{16,20},{20,24},{24,28},{1,5},{5,9},{9,... | collective-permute-start | bytes 24584 | tf_op jit(solution)/shard_map/ppermute | solution.py:21
  249.2 10.3 %collective-permute-start.35 = (f32[8,6,1,32]{0,3,2,1:T(8,128)}, f32[8,6,1,32]{0,3,2,1:T(8,128)}, u32[]{:S(2)}, u32[]{:S(2)}) collective-permute-start(f32[8,6,1,32]{0,3,2,1:T(8,128)} %get-tuple-element.64), channel_id=1, source_target_pairs={{0,1},{1,2},{2,3},{4,5},{5,6},{6,7},{8,9},{9,10},{10,11},{12,13},{... | collective-permute-start | bytes 18440 | tf_op jit(solution)/shard_map/ppermute | solution.py:21
  254.6 7.2 %collective-permute-start.34 = (f32[8,6,1,32]{0,3,2,1:T(8,128)}, f32[8,6,1,32]{0,3,2,1:T(8,128)}, u32[]{:S(2)}, u32[]{:S(2)}) collective-permute-start(f32[8,6,1,32]{0,3,2,1:T(8,128)} %get-tuple-element.63), channel_id=1, source_target_pairs={{1,0},{2,1},{3,2},{5,4},{6,5},{7,6},{9,8},{10,9},{11,10},{13,12},{... | collective-permute-start | bytes 18440 | tf_op jit(solution)/shard_map/ppermute | solution.py:23
  268.5 25.9 %collective-permute-start.40 = (f32[8,1,4,16]{0,3,2,1:T(8,128)}, f32[8,1,4,16]{0,3,2,1:T(8,128)}, u32[]{:S(2)}, u32[]{:S(2)}) collective-permute-start(f32[8,1,4,16]{0,3,2,1:T(8,128)} %get-tuple-element.112), channel_id=1, source_target_pairs={{4,0},{8,4},{12,8},{16,12},{20,16},{24,20},{28,24},{5,1},{9,5},{13... | collective-permute-start | bytes 6152 | tf_op jit(solution)/shard_map/ppermute | solution.py:23
  270.4 24.0 %collective-permute-start.41 = (f32[8,1,4,16]{0,3,2,1:T(8,128)}, f32[8,1,4,16]{0,3,2,1:T(8,128)}, u32[]{:S(2)}, u32[]{:S(2)}) collective-permute-start(f32[8,1,4,16]{0,3,2,1:T(8,128)} %get-tuple-element.111), channel_id=1, source_target_pairs={{0,4},{4,8},{8,12},{12,16},{16,20},{20,24},{24,28},{1,5},{5,9},{9,... | collective-permute-start | bytes 6152 | tf_op jit(solution)/shard_map/ppermute | solution.py:21
  295.2 5.3 collective-permute-start.43
  298.5 5.8 %collective-permute-start.42 = (f32[8,4,1,16]{0,3,2,1:T(8,128)S(1)}, f32[8,4,1,16]{0,3,2,1:T(8,128)S(1)}, u32[]{:S(2)}, u32[]{:S(2)}) collective-permute-start(f32[8,4,1,16]{0,3,2,1:T(8,128)S(1)} %get-tuple-element.101), channel_id=1, source_target_pairs={{1,0},{2,1},{3,2},{5,4},{6,5},{7,6},{9,8},{10,9},{11,10},{13,12},{... | collective-permute-start | bytes 6152 | tf_op jit(solution)/shard_map/ppermute | solution.py:23
  314.1 6.2 %collective-permute-start.47 = (f32[8,4,1,16]{0,3,2,1:T(8,128)S(1)}, f32[8,4,1,16]{0,3,2,1:T(8,128)S(1)}, u32[]{:S(2)}, u32[]{:S(2)}) collective-permute-start(f32[8,4,1,16]{0,3,2,1:T(8,128)S(1)} %get-tuple-element.100), channel_id=1, source_target_pairs={{0,1},{1,2},{2,3},{4,5},{5,6},{6,7},{8,9},{9,10},{10,11},{12,13},{... | collective-permute-start | bytes 6152 | tf_op jit(solution)/shard_map/ppermute | solution.py:21
  318.4 5.8 %collective-permute-start.46 = (f32[8,4,1,16]{0,3,2,1:T(8,128)S(1)}, f32[8,4,1,16]{0,3,2,1:T(8,128)S(1)}, u32[]{:S(2)}, u32[]{:S(2)}) collective-permute-start(f32[8,4,1,16]{0,3,2,1:T(8,128)S(1)} %get-tuple-element.99), channel_id=1, source_target_pairs={{1,0},{2,1},{3,2},{5,4},{6,5},{7,6},{9,8},{10,9},{11,10},{13,12},{... | collective-permute-start | bytes 6152 | tf_op jit(solution)/shard_map/ppermute | solution.py:23
  356.4 6.5 %collective-permute-start.48 = (f32[8,1,4,16]{0,3,2,1:T(8,128)S(1)}, f32[8,1,4,16]{0,3,2,1:T(8,128)S(1)}, u32[]{:S(2)}, u32[]{:S(2)}) collective-permute-start(f32[8,1,4,16]{0,3,2,1:T(8,128)S(1)} %get-tuple-element.108), channel_id=1, source_target_pairs={{4,0},{8,4},{12,8},{16,12},{20,16},{24,20},{28,24},{5,1},{9,5},{13... | collective-permute-start | bytes 6152 | tf_op jit(solution)/shard_map/ppermute | solution.py:23
  361.0 5.2 collective-permute-start.49
  369.3 5.8 %collective-permute-start.50 = (f32[8,4,1,16]{0,3,2,1:T(8,128)S(1)}, f32[8,4,1,16]{0,3,2,1:T(8,128)S(1)}, u32[]{:S(2)}, u32[]{:S(2)}) collective-permute-start(f32[8,4,1,16]{0,3,2,1:T(8,128)S(1)} %get-tuple-element.97), channel_id=1, source_target_pairs={{1,0},{2,1},{3,2},{5,4},{6,5},{7,6},{9,8},{10,9},{11,10},{13,12},{... | collective-permute-start | bytes 6152 | tf_op jit(solution)/shard_map/ppermute | solution.py:23
  378.2 5.4 collective-permute-start.53
  383.5 5.9 %collective-permute-start.55 = (f32[8,4,1,16]{0,3,2,1:T(8,128)S(1)}, f32[8,4,1,16]{0,3,2,1:T(8,128)S(1)}, u32[]{:S(2)}, u32[]{:S(2)}) collective-permute-start(f32[8,4,1,16]{0,3,2,1:T(8,128)S(1)} %get-tuple-element.96), channel_id=1, source_target_pairs={{0,1},{1,2},{2,3},{4,5},{5,6},{6,7},{8,9},{9,10},{10,11},{12,13},{... | collective-permute-start | bytes 6152 | tf_op jit(solution)/shard_map/ppermute | solution.py:21
  387.8 5.8 %collective-permute-start.54 = (f32[8,4,1,16]{0,3,2,1:T(8,128)S(1)}, f32[8,4,1,16]{0,3,2,1:T(8,128)S(1)}, u32[]{:S(2)}, u32[]{:S(2)}) collective-permute-start(f32[8,4,1,16]{0,3,2,1:T(8,128)S(1)} %get-tuple-element.95), channel_id=1, source_target_pairs={{1,0},{2,1},{3,2},{5,4},{6,5},{7,6},{9,8},{10,9},{11,10},{13,12},{... | collective-permute-start | bytes 6152 | tf_op jit(solution)/shard_map/ppermute | solution.py:23
  397.0 6.3 %collective-permute-start.57 = (f32[8,1,8,32]{0,3,2,1:T(8,128)S(1)}, f32[8,1,8,32]{0,3,2,1:T(8,128)S(1)}, u32[]{:S(2)}, u32[]{:S(2)}) collective-permute-start(f32[8,1,8,32]{0,3,2,1:T(8,128)S(1)} %get-tuple-element.81), channel_id=1, source_target_pairs={{0,4},{4,8},{8,12},{12,16},{16,20},{20,24},{24,28},{1,5},{5,9},{9,... | collective-permute-start | bytes 24584 | tf_op jit(solution)/shard_map/ppermute | solution.py:21
  406.1 6.5 %collective-permute-start.58 = (f32[8,6,1,32]{0,3,2,1:T(8,128)S(1)}, f32[8,6,1,32]{0,3,2,1:T(8,128)S(1)}, u32[]{:S(2)}, u32[]{:S(2)}) collective-permute-start(f32[8,6,1,32]{0,3,2,1:T(8,128)S(1)} %get-tuple-element.61), channel_id=1, source_target_pairs={{1,0},{2,1},{3,2},{5,4},{6,5},{7,6},{9,8},{10,9},{11,10},{13,12},{... | collective-permute-start | bytes 18440 | tf_op jit(solution)/shard_map/ppermute | solution.py:23
  416.2 6.3 %collective-permute-start.61 = (f32[8,1,8,32]{0,3,2,1:T(8,128)S(1)}, f32[8,1,8,32]{0,3,2,1:T(8,128)S(1)}, u32[]{:S(2)}, u32[]{:S(2)}) collective-permute-start(f32[8,1,8,32]{0,3,2,1:T(8,128)S(1)} %get-tuple-element.79), channel_id=1, source_target_pairs={{0,4},{4,8},{8,12},{12,16},{16,20},{20,24},{24,28},{1,5},{5,9},{9,... | collective-permute-start | bytes 24584 | tf_op jit(solution)/shard_map/ppermute | solution.py:21
  425.3 6.5 %collective-permute-start.62 = (f32[8,6,1,32]{0,3,2,1:T(8,128)S(1)}, f32[8,6,1,32]{0,3,2,1:T(8,128)S(1)}, u32[]{:S(2)}, u32[]{:S(2)}) collective-permute-start(f32[8,6,1,32]{0,3,2,1:T(8,128)S(1)} %get-tuple-element.59), channel_id=1, source_target_pairs={{1,0},{2,1},{3,2},{5,4},{6,5},{7,6},{9,8},{10,9},{11,10},{13,12},{... | collective-permute-start | bytes 18440 | tf_op jit(solution)/shard_map/ppermute | solution.py:23
  444.4 5.6 collective-permute-start.65
  452.9 5.9 %collective-permute-start.66 = (f32[8,10,1,64]{3,2,1,0:T(1,128)S(1)}, f32[8,10,1,64]{3,2,1,0:T(1,128)S(1)}, u32[]{:S(2)}, u32[]{:S(2)}) collective-permute-start(f32[8,10,1,64]{3,2,1,0:T(1,128)S(1)} %get-tuple-element.69), channel_id=1, source_target_pairs={{1,0},{2,1},{3,2},{5,4},{6,5},{7,6},{9,8},{10,9},{11,10},{13,12},{... | collective-permute-start | bytes 61448 | tf_op jit(solution)/shard_map/ppermute | solution.py:23
  461.4 5.6 collective-permute-start.69
  469.9 5.9 %collective-permute-start.70 = (f32[8,10,1,64]{3,2,1,0:T(1,128)S(1)}, f32[8,10,1,64]{3,2,1,0:T(1,128)S(1)}, u32[]{:S(2)}, u32[]{:S(2)}) collective-permute-start(f32[8,10,1,64]{3,2,1,0:T(1,128)S(1)} %get-tuple-element.67), channel_id=1, source_target_pairs={{1,0},{2,1},{3,2},{5,4},{6,5},{7,6},{9,8},{10,9},{11,10},{13,12},{... | collective-permute-start | bytes 61448 | tf_op jit(solution)/shard_map/ppermute | solution.py:23
  521.7 6.3 %collective-permute-start.73 = (f32[8,1,32,128]{3,2,1,0:T(8,128)S(1)}, f32[8,1,32,128]{3,2,1,0:T(8,128)S(1)}, u32[]{:S(2)}, u32[]{:S(2)}) collective-permute-start(f32[8,1,32,128]{3,2,1,0:T(8,128)S(1)} %get-tuple-element.53), channel_id=1, source_target_pairs={{0,4},{4,8},{8,12},{12,16},{16,20},{20,24},{24,28},{1,5},{5,9},{9,... | collective-permute-start | bytes 393224 | tf_op jit(solution)/shard_map/ppermute | solution.py:21
  531.0 6.2 %collective-permute-start.74 = (f32[8,18,1,128]{3,0,2,1:T(8,128)S(1)}, f32[8,18,1,128]{3,0,2,1:T(8,128)S(1)}, u32[]{:S(2)}, u32[]{:S(2)}) collective-permute-start(f32[8,18,1,128]{3,0,2,1:T(8,128)S(1)} %copy.534), channel_id=1, source_target_pairs={{1,0},{2,1},{3,2},{5,4},{6,5},{7,6},{9,8},{10,9},{11,10},{13,12},{... | collective-permute-start | bytes 221192 | tf_op jit(solution)/shard_map/ppermute | solution.py:23
  542.9 6.3 %collective-permute-start.77 = (f32[8,1,32,128]{3,2,1,0:T(8,128)S(1)}, f32[8,1,32,128]{3,2,1,0:T(8,128)S(1)}, u32[]{:S(2)}, u32[]{:S(2)}) collective-permute-start(f32[8,1,32,128]{3,2,1,0:T(8,128)S(1)} %get-tuple-element.51), channel_id=1, source_target_pairs={{0,4},{4,8},{8,12},{12,16},{16,20},{20,24},{24,28},{1,5},{5,9},{9,... | collective-permute-start | bytes 393224 | tf_op jit(solution)/shard_map/ppermute | solution.py:21
  552.2 6.2 %collective-permute-start.78 = (f32[8,18,1,128]{3,0,2,1:T(8,128)S(1)}, f32[8,18,1,128]{3,0,2,1:T(8,128)S(1)}, u32[]{:S(2)}, u32[]{:S(2)}) collective-permute-start(f32[8,18,1,128]{3,0,2,1:T(8,128)S(1)} %copy.538), channel_id=1, source_target_pairs={{1,0},{2,1},{3,2},{5,4},{6,5},{7,6},{9,8},{10,9},{11,10},{13,12},{... | collective-permute-start | bytes 221192 | tf_op jit(solution)/shard_map/ppermute | solution.py:23
  (107 other events, 2187.1 us)
where the time goes:
time: 574 us; the launch traced here: 563 us
  starting transfers between devices  202 us (35%)
  other arithmetic  116 us (20%)
  local copies, waits for them, and re-layouts  106 us (18%)
  waiting for transfers between devices  96.2 us (17%)
  blocking collectives  41.1 us (7%)
    ppermute x40, starting transfers between devices, padded(): lax.ppermute(tail, axis, [(i, (i + 1) % count) for i in range(ends)])  128 us
    ppermute x40, starting transfers between devices, padded(): lax.ppermute(head, axis, [((i + 1) % count, i) for i in range(ends)])  73.2 us
    ppermute x40, waiting for transfers between devices, padded(): lax.ppermute(head, axis, [((i + 1) % count, i) for i in range(ends)])  52.2 us
    ppermute x40, waiting for transfers between devices, padded(): lax.ppermute(tail, axis, [(i, (i + 1) % count) for i in range(ends)])  44.1 us
    reduce_sum x5, other arithmetic, restrict_sum(): field.reshape(rr, sx // 2, 2, sy // 2, 2, sz // 2, 2).sum(axis=(2, 4, 6))  33.5 us
    add x25, other arithmetic, relax(): field + damping * (source - apply_operator(padder(field), field, coeffs,...  30.3 us
    reshape x2, local copies, waits for them, and re-layouts, prolong_copy(): return grown.reshape(rr, 2 * sx, 2 * sy, 2 * sz)  23.7 us
    sub x2, local copies, waits for them, and re-layouts, local(): source - apply_operator(field_rim(field), field, coeffs, face_sum, scale)  20.7 us
  transfers between devices with their start and end apart: 80, of which 39 were waited for; matrix products, arithmetic and copies ran while one was open for 20% of the time, Pallas kernels for 0%

commit v1 on v0

--- a/solution.py
+++ b/solution.py
@@ -1,3 +1,4 @@
+import functools
 import jax
 import jax.numpy as jnp
 from jax import lax
@@ -8,6 +9,25 @@
 COARSE_SWEEPS = 16
 CLASSES = 6
 damping = 0.8
+
+
+def _finish_axis_part(row_data, which_axis):
+    n_slots = lax.axis_size(which_axis)
+    vals = [(kk, (kk + 1) % n_slots) for kk in range(n_slots)]
+    gallery = [(kk, (kk - 1) % n_slots) for kk in range(n_slots)]
+    finding, mixed_arr = ([row_data], [row_data])
+    for _ in range(n_slots // 2):
+        w1 = lax.ppermute(finding[-1], perm=vals, axis_name=which_axis)
+        finding.append(w1)
+    for _ in tuple(range((n_slots - 1) // 2)):
+        shaped = lax.ppermute(mixed_arr[-1], perm=gallery, axis_name=which_axis)
+        mixed_arr.append(shaped)
+    piece_out = jnp.concatenate([*finding[::-1], *mixed_arr[1:]], axis=1)
+    a_now = lax.axis_index(which_axis)
+    return jnp.roll(piece_out, (a_now - n_slots // 2) * row_data.shape[1], 1)
+
+
+store_body_in = functools.partial(_finish_axis_part, which_axis="gx")
 
 
 def padded(cells, sides, width):
@@ -142,7 +162,7 @@
         lax.all_gather(conductivities[depth], "gy", axis=1, tiled=True),
     )
     gathered, coarse_cond = (
-        lax.all_gather(gathered, "gx", axis=1, tiled=True),
+        store_body_in(gathered),
         lax.all_gather(coarse_cond, "gx", axis=0, tiled=True),
     )
     coarse_list = [coarse_cond]

time: 574 us -> 575 us (level)
  the two profiles are of different devices: /device:TPU:16 before, /device:TPU:8 now
where the time goes in v1:
time: 575 us; the launch traced here: 564 us
  starting transfers between devices  203 us (35%)
  other arithmetic  110 us (19%)
  local copies, waits for them, and re-layouts  109 us (19%)
  waiting for transfers between devices  108 us (19%)
  blocking collectives  30.6 us (5%)
    ppermute x40, starting transfers between devices, padded(): lax.ppermute(tail, axis, [(i, (i + 1) % count) for i in range(ends)])  127 us
    ppermute x40, starting transfers between devices, padded(): lax.ppermute(head, axis, [((i + 1) % count, i) for i in range(ends)])  71 us
    ppermute x40, waiting for transfers between devices, padded(): lax.ppermute(head, axis, [((i + 1) % count, i) for i in range(ends)])  52.7 us
    ppermute x40, waiting for transfers between devices, padded(): lax.ppermute(tail, axis, [(i, (i + 1) % count) for i in range(ends)])  50.8 us
    reduce_sum x5, other arithmetic, restrict_sum(): field.reshape(rr, sx // 2, 2, sy // 2, 2, sz // 2, 2).sum(axis=(2, 4, 6))  34.4 us
    add x25, other arithmetic, relax(): field + damping * (source - apply_operator(padder(field), field, coeffs,...  26.6 us
    reshape x2, local copies, waits for them, and re-layouts, prolong_copy(): return grown.reshape(rr, 2 * sx, 2 * sy, 2 * sz)  23.7 us
    broadcast_in_dim x5, local copies, waits for them, and re-layouts, prolong_copy(): jnp.broadcast_to(field[:, :, None, :, None, :, None], (rr, sx, 2, sy, 2,...  22.5 us
  transfers between devices with their start and end apart: 87, of which 47 were waited for; matrix products, arithmetic and copies ran while one was open for 20% of the time, Pallas kernels for 0%

profile of v1, /device:TPU:8, one launch (start us, length us, event | category | flops | bytes accessed | tf_op | source)
XLA Modules:
  0.0 563.8 jit_solution(11005918562014356223)
XLA Ops:
  1.5 4.7 select_add_fusion
  8.2 3.6 collective-permute-start
  11.9 18.1 %reshape.94 = f32[8,2,16,2,64,2]{5,4,3,2,1,0:T(8,128)} reshape(f32[16,32,128]{2,1,0:T(8,128)S(1)} %select_add_fusion) | data formatting | bytes 524288 | tf_op jit(solution)/shard_map/reshape | solution.py:59
  30.0 7.0 %reduce_sum.89 = f32[8,16,64]{2,1,0:T(8,128)S(1)} reduce(f32[8,2,16,2,64,2]{5,4,3,2,1,0:T(8,128)} %reshape.94, f32[]{:T(128)} %constant.90.clone.1), dimensions={1,3,5}, to_apply=%region_1.2 | reduce | flops 57344 | bytes 294916 | tf_op jit(solution)/shard_map/reduce_sum | solution.py:59
  39.6 3.6 collective-permute-start.12
  43.2 3.5 div.336
  50.0 4.5 collective-permute-start.3
  55.9 3.2 add_add_fusion
  66.4 3.1 collective-permute-start.25
  76.1 4.3 collective-permute-start.7
  83.1 6.3 %collective-permute-start.15 = (f32[10,1,64]{2,1,0:T(1,128)S(1)}, f32[10,1,64]{2,1,0:T(1,128)S(1)}, u32[]{:S(2)}, u32[]{:S(2)}) collective-permute-start(f32[10,1,64]{2,1,0:T(1,128)S(1)} %get-tuple-element.103), channel_id=1, source_target_pairs={{0,1},{1,2},{2,3},{4,5},{5,6},{6,7},{8,9},{9,10},{10,11},{12,13},{... | collective-permute-start | bytes 7688 | tf_op jit(solution)/shard_map/ppermute | solution.py:41
  89.7 4.6 fusion.7
  102.7 4.8 collective-permute-start.11
  110.0 3.7 collective-permute-done.10
  113.9 4.4 fusion.13
  118.3 18.0 %copy.522 = f32[8,16,32,128]{0,3,2,1:T(8,128)} copy(f32[8,16,32,128]{3,2,1,0:T(8,128)} %fusion.13) | data formatting | bytes 4194304 | tf_op jit(solution)/shard_map/sub | solution.py:155
  136.2 24.2 %reduce_sum.88 = f32[8,8,16,64]{0,3,2,1:T(8,128)} reduce(f32[8,8,2,16,2,64,2]{0,6,5,4,3,2,1:T(2,128)} %bitcast.23, f32[]{:T(128)} %constant.90.clone.1), dimensions={2,4,6}, to_apply=%region_0.1 | reduce | flops 458752 | bytes 2359300 | tf_op jit(solution)/shard_map/reduce_sum | solution.py:64
  160.5 2.9 copy.523
  172.0 4.8 collective-permute-start.19
  180.2 5.2 collective-permute-start.27
  193.8 4.8 collective-permute-start.23
  200.5 3.9 collective-permute-done.22
  207.8 4.8 reduce_sum.90
  218.8 3.1 collective-permute-start.37
  224.4 2.8 collective-permute-start.31
  229.8 5.2 collective-permute-start.39
  244.9 4.8 collective-permute-start.35
  251.9 4.3 collective-permute-done.34
  272.9 4.2 collective-permute-done.42
  283.7 3.1 collective-permute-done.45
  288.3 3.4 collective-permute-start.47
  302.5 8.5 %all-gather = f32[8,8,8]{2,0,1:T(8,128)} all-gather(f32[8,2,8]{2,0,1:T(8,128)} %copy.527), channel_id=2, replica_groups=mesh['gx'=8,'gy'=4] {'gy'}, dimensions={1}, use_global_device_ids=true | all-gather | bytes 2560 | tf_op jit(solution)/shard_map/all_gather | solution.py:161
  312.4 7.3 %all-gather.3 = f32[4,2,8]{2,1,0:T(2,128)S(1)} all-gather(f32[1,2,8]{2,1,0:T(2,128)} %multiply_bitcast_fusion), channel_id=3, replica_groups=mesh['gx'=8,'gy'=4] {'gy'}, dimensions={0}, use_global_device_ids=true | all-gather | bytes 320 | tf_op jit(solution)/shard_map/all_gather | solution.py:162
  319.7 14.8 %all-gather.2 = f32[64,8]{1,0:T(8,128)S(1)} all-gather(f32[8,8]{1,0:T(8,128)S(1)} %bitcast.32), channel_id=4, replica_groups=mesh['gx'=8,'gy'=4] {'gx'}, dimensions={0}, use_global_device_ids=true | all-gather | bytes 2304 | tf_op jit(solution)/shard_map/all_gather | solution.py:166
  355.7 3.2 collective-permute-start.55
  360.8 6.0 %collective-permute-done.56 = f32[8,1,4,16]{0,3,2,1:T(8,128)S(1)} collective-permute-done((f32[8,1,4,16]{0,3,2,1:T(8,128)S(1)}, f32[8,1,4,16]{0,3,2,1:T(8,128)S(1)}, u32[]{:S(2)}, u32[]{:S(2)}) %collective-permute-start.56) | collective-permute-done | bytes 2080 | tf_op jit(solution)/shard_map/ppermute | solution.py:41
  366.8 3.2 collective-permute-start.58
  371.6 4.2 collective-permute-done.57
  384.3 4.3 collective-permute-start.62
  390.2 4.2 collective-permute-done.61
  400.3 3.8 collective-permute-done.64
  404.1 2.8 collective-permute-start.66
  409.1 4.3 collective-permute-done.65
  419.4 3.8 collective-permute-done.68
  423.2 2.8 collective-permute-start.70
  428.3 4.3 collective-permute-done.69
  434.1 4.2 broadcast_in_dim.54
  438.2 3.6 copy.529
  447.5 3.2 collective-permute-done.72
  455.2 4.2 collective-permute-done.73
  464.5 3.2 collective-permute-done.76
  467.7 2.8 collective-permute-start.78
  472.2 4.2 collective-permute-done.77
  477.8 3.6 copy.532
  481.4 16.0 %broadcast_in_dim.55 = f32[8,8,2,16,2,64,2]{0,6,5,4,3,2,1:T(2,128)} broadcast(f32[8,8,16,64]{0,3,2,1:T(8,128)} %copy.532), dimensions={0,1,3,5} | broadcast | bytes 2359296 | tf_op jit(solution)/shard_map/broadcast_in_dim | solution.py:69
  497.4 20.1 %copy.533 = f32[8,16,32,128]{3,2,1,0:T(8,128)} copy(f32[8,16,32,128]{0,3,2,1:T(8,128)} %bitcast.24) | data formatting | bytes 4194304 | tf_op jit(solution)/shard_map/reshape | solution.py:70
  524.8 3.8 collective-permute-done.80
  528.7 2.8 collective-permute-start.82
  533.6 4.2 collective-permute-done.81
  538.0 3.6 fusion.22
  546.0 3.8 collective-permute-done.84
  549.9 2.8 collective-permute-start.86
  554.8 4.2 collective-permute-done.85
  559.1 4.5 fusion.31
  (416 shorter events, 209.5 us)
Async XLA Ops:
  6.3 42.4 %collective-permute-start.1 = (f32[1,32,128]{2,1,0:T(8,128)S(1)}, f32[1,32,128]{2,1,0:T(8,128)S(1)}, u32[]{:S(2)}, u32[]{:S(2)}) collective-permute-start(f32[1,32,128]{2,1,0:T(8,128)S(1)} %get-tuple-element.94), channel_id=1, source_target_pairs={{0,4},{4,8},{8,12},{12,16},{16,20},{20,24},{24,28},{1,5},{5,9},{9,... | collective-permute-start | bytes 49160 | tf_op jit(solution)/shard_map/ppermute | solution.py:41
  8.2 40.5 %collective-permute-start = (f32[1,32,128]{2,1,0:T(8,128)S(1)}, f32[1,32,128]{2,1,0:T(8,128)S(1)}, u32[]{:S(2)}, u32[]{:S(2)}) collective-permute-start(f32[1,32,128]{2,1,0:T(8,128)S(1)} %get-tuple-element.93), channel_id=1, source_target_pairs={{4,0},{8,4},{12,8},{16,12},{20,16},{24,20},{28,24},{5,1},{9,5},{13... | collective-permute-start | bytes 49160 | tf_op jit(solution)/shard_map/ppermute | solution.py:43
  37.6 42.8 %collective-permute-start.13 = (f32[1,16,64]{2,1,0:T(8,128)}, f32[1,16,64]{2,1,0:T(8,128)S(1)}, u32[]{:S(2)}, u32[]{:S(2)}) collective-permute-start(f32[1,16,64]{2,1,0:T(8,128)} %get-tuple-element.114), channel_id=1, source_target_pairs={{0,4},{4,8},{8,12},{12,16},{16,20},{20,24},{24,28},{1,5},{5,9},{9,... | collective-permute-start | bytes 12296 | tf_op jit(solution)/shard_map/ppermute | solution.py:41
  39.6 42.2 %collective-permute-start.12 = (f32[1,16,64]{2,1,0:T(8,128)}, f32[1,16,64]{2,1,0:T(8,128)S(1)}, u32[]{:S(2)}, u32[]{:S(2)}) collective-permute-start(f32[1,16,64]{2,1,0:T(8,128)} %get-tuple-element.113), channel_id=1, source_target_pairs={{4,0},{8,4},{12,8},{16,12},{20,16},{24,20},{28,24},{5,1},{9,5},{13... | collective-permute-start | bytes 12296 | tf_op jit(solution)/shard_map/ppermute | solution.py:43
  48.7 5.9 %collective-permute-start.2 = (f32[18,1,128]{2,1,0:T(1,128)S(1)}, f32[18,1,128]{2,1,0:T(1,128)S(1)}, u32[]{:S(2)}, u32[]{:S(2)}) collective-permute-start(f32[18,1,128]{2,1,0:T(1,128)S(1)} %get-tuple-element.92), channel_id=1, source_target_pairs={{1,0},{2,1},{3,2},{5,4},{6,5},{7,6},{9,8},{10,9},{11,10},{13,12},{... | collective-permute-start | bytes 27656 | tf_op jit(solution)/shard_map/ppermute | solution.py:43
  50.0 5.9 %collective-permute-start.3 = (f32[18,1,128]{2,1,0:T(1,128)S(1)}, f32[18,1,128]{2,1,0:T(1,128)S(1)}, u32[]{:S(2)}, u32[]{:S(2)}) collective-permute-start(f32[18,1,128]{2,1,0:T(1,128)S(1)} %get-tuple-element.91), channel_id=1, source_target_pairs={{0,1},{1,2},{2,3},{4,5},{5,6},{6,7},{8,9},{9,10},{10,11},{12,13},{... | collective-permute-start | bytes 27656 | tf_op jit(solution)/shard_map/ppermute | solution.py:41
  61.5 10.6 %collective-permute-start.4 = (f32[8,1,32,128]{3,2,1,0:T(8,128)}, f32[8,1,32,128]{3,2,1,0:T(8,128)}, u32[]{:S(2)}, u32[]{:S(2)}) collective-permute-start(f32[8,1,32,128]{3,2,1,0:T(8,128)} %get-tuple-element.58), channel_id=1, source_target_pairs={{4,0},{8,4},{12,8},{16,12},{20,16},{24,20},{28,24},{5,1},{9,5},{13... | collective-permute-start | bytes 393224 | tf_op jit(solution)/shard_map/ppermute | solution.py:43
  63.4 11.3 %collective-permute-start.5 = (f32[8,1,32,128]{3,2,1,0:T(8,128)}, f32[8,1,32,128]{3,2,1,0:T(8,128)}, u32[]{:S(2)}, u32[]{:S(2)}) collective-permute-start(f32[8,1,32,128]{3,2,1,0:T(8,128)} %get-tuple-element.57), channel_id=1, source_target_pairs={{0,4},{4,8},{8,12},{12,16},{16,20},{20,24},{24,28},{1,5},{5,9},{9,... | collective-permute-start | bytes 393224 | tf_op jit(solution)/shard_map/ppermute | solution.py:41
  66.4 111.7 %collective-permute-start.25 = (f32[1,8,32]{2,1,0:T(8,128)}, f32[1,8,32]{2,1,0:T(8,128)}, u32[]{:S(2)}, u32[]{:S(2)}) collective-permute-start(f32[1,8,32]{2,1,0:T(8,128)} %get-tuple-element.118), channel_id=1, source_target_pairs={{0,4},{4,8},{8,12},{12,16},{16,20},{20,24},{24,28},{1,5},{5,9},{9,... | collective-permute-start | bytes 3080 | tf_op jit(solution)/shard_map/ppermute | solution.py:41
  72.1 106.1 %collective-permute-start.24 = (f32[1,8,32]{2,1,0:T(8,128)}, f32[1,8,32]{2,1,0:T(8,128)}, u32[]{:S(2)}, u32[]{:S(2)}) collective-permute-start(f32[1,8,32]{2,1,0:T(8,128)} %get-tuple-element.117), channel_id=1, source_target_pairs={{4,0},{8,4},{12,8},{16,12},{20,16},{24,20},{28,24},{5,1},{9,5},{13... | collective-permute-start | bytes 3080 | tf_op jit(solution)/shard_map/ppermute | solution.py:43
  76.1 7.0 %collective-permute-start.7 = (f32[8,18,1,128]{3,0,2,1:T(8,128)S(1)}, f32[8,18,1,128]{3,0,2,1:T(8,128)S(1)}, u32[]{:S(2)}, u32[]{:S(2)}) collective-permute-start(f32[8,18,1,128]{3,0,2,1:T(8,128)S(1)} %copy.516), channel_id=1, source_target_pairs={{0,1},{1,2},{2,3},{4,5},{5,6},{6,7},{8,9},{9,10},{10,11},{12,13},{... | collective-permute-start | bytes 221192 | tf_op jit(solution)/shard_map/ppermute | solution.py:41
  80.4 9.1 %collective-permute-start.6 = (f32[8,18,1,128]{3,0,2,1:T(8,128)S(1)}, f32[8,18,1,128]{3,0,2,1:T(8,128)S(1)}, u32[]{:S(2)}, u32[]{:S(2)}) collective-permute-start(f32[8,18,1,128]{3,0,2,1:T(8,128)S(1)} %copy.514), channel_id=1, source_target_pairs={{1,0},{2,1},{3,2},{5,4},{6,5},{7,6},{9,8},{10,9},{11,10},{13,12},{... | collective-permute-start | bytes 221192 | tf_op jit(solution)/shard_map/ppermute | solution.py:43
  81.8 14.5 %collective-permute-start.14 = (f32[10,1,64]{2,1,0:T(1,128)S(1)}, f32[10,1,64]{2,1,0:T(1,128)S(1)}, u32[]{:S(2)}, u32[]{:S(2)}) collective-permute-start(f32[10,1,64]{2,1,0:T(1,128)S(1)} %get-tuple-element.104), channel_id=1, source_target_pairs={{1,0},{2,1},{3,2},{5,4},{6,5},{7,6},{9,8},{10,9},{11,10},{13,12},{... | collective-permute-start | bytes 7688 | tf_op jit(solution)/shard_map/ppermute | solution.py:43
  83.1 15.6 %collective-permute-start.15 = (f32[10,1,64]{2,1,0:T(1,128)S(1)}, f32[10,1,64]{2,1,0:T(1,128)S(1)}, u32[]{:S(2)}, u32[]{:S(2)}) collective-permute-start(f32[10,1,64]{2,1,0:T(1,128)S(1)} %get-tuple-element.103), channel_id=1, source_target_pairs={{0,1},{1,2},{2,3},{4,5},{5,6},{6,7},{8,9},{9,10},{10,11},{12,13},{... | collective-permute-start | bytes 7688 | tf_op jit(solution)/shard_map/ppermute | solution.py:41
  94.3 5.9 %collective-permute-start.8 = (f32[8,1,32,128]{3,2,1,0:T(8,128)S(1)}, f32[8,1,32,128]{3,2,1,0:T(8,128)S(1)}, u32[]{:S(2)}, u32[]{:S(2)}) collective-permute-start(f32[8,1,32,128]{3,2,1,0:T(8,128)S(1)} %get-tuple-element.56), channel_id=1, source_target_pairs={{4,0},{8,4},{12,8},{16,12},{20,16},{24,20},{28,24},{5,1},{9,5},{13... | collective-permute-start | bytes 393224 | tf_op jit(solution)/shard_map/ppermute | solution.py:43
  96.3 6.3 %collective-permute-start.9 = (f32[8,1,32,128]{3,2,1,0:T(8,128)S(1)}, f32[8,1,32,128]{3,2,1,0:T(8,128)S(1)}, u32[]{:S(2)}, u32[]{:S(2)}) collective-permute-start(f32[8,1,32,128]{3,2,1,0:T(8,128)S(1)} %get-tuple-element.55), channel_id=1, source_target_pairs={{0,4},{4,8},{8,12},{12,16},{16,20},{20,24},{24,28},{1,5},{5,9},{9,... | collective-permute-start | bytes 393224 | tf_op jit(solution)/shard_map/ppermute | solution.py:41
  102.7 7.3 %collective-permute-start.11 = (f32[8,18,1,128]{3,0,2,1:T(8,128)S(1)}, f32[8,18,1,128]{3,0,2,1:T(8,128)S(1)}, u32[]{:S(2)}, u32[]{:S(2)}) collective-permute-start(f32[8,18,1,128]{3,0,2,1:T(8,128)S(1)} %copy.520), channel_id=1, source_target_pairs={{0,1},{1,2},{2,3},{4,5},{5,6},{6,7},{8,9},{9,10},{10,11},{12,13},{... | collective-permute-start | bytes 221192 | tf_op jit(solution)/shard_map/ppermute | solution.py:41
  107.5 6.2 %collective-permute-start.10 = (f32[8,18,1,128]{3,0,2,1:T(8,128)S(1)}, f32[8,18,1,128]{3,0,2,1:T(8,128)S(1)}, u32[]{:S(2)}, u32[]{:S(2)}) collective-permute-start(f32[8,18,1,128]{3,0,2,1:T(8,128)S(1)} %copy.518), channel_id=1, source_target_pairs={{1,0},{2,1},{3,2},{5,4},{6,5},{7,6},{9,8},{10,9},{11,10},{13,12},{... | collective-permute-start | bytes 221192 | tf_op jit(solution)/shard_map/ppermute | solution.py:43
  164.4 5.6 collective-permute-start.16
  166.4 5.6 collective-permute-start.17
  172.0 13.4 %collective-permute-start.19 = (f32[8,10,1,64]{3,2,1,0:T(1,128)S(1)}, f32[8,10,1,64]{3,2,1,0:T(1,128)S(1)}, u32[]{:S(2)}, u32[]{:S(2)}) collective-permute-start(f32[8,10,1,64]{3,2,1,0:T(1,128)S(1)} %get-tuple-element.74), channel_id=1, source_target_pairs={{0,1},{1,2},{2,3},{4,5},{5,6},{6,7},{8,9},{9,10},{10,11},{12,13},{... | collective-permute-start | bytes 61448 | tf_op jit(solution)/shard_map/ppermute | solution.py:41
  176.8 8.6 %collective-permute-start.18 = (f32[8,10,1,64]{3,2,1,0:T(1,128)S(1)}, f32[8,10,1,64]{3,2,1,0:T(1,128)S(1)}, u32[]{:S(2)}, u32[]{:S(2)}) collective-permute-start(f32[8,10,1,64]{3,2,1,0:T(1,128)S(1)} %get-tuple-element.73), channel_id=1, source_target_pairs={{1,0},{2,1},{3,2},{5,4},{6,5},{7,6},{9,8},{10,9},{11,10},{13,12},{... | collective-permute-start | bytes 61448 | tf_op jit(solution)/shard_map/ppermute | solution.py:43
  178.9 11.6 %collective-permute-start.26 = (f32[6,1,32]{2,1,0:T(1,128)S(1)}, f32[6,1,32]{2,1,0:T(1,128)S(1)}, u32[]{:S(2)}, u32[]{:S(2)}) collective-permute-start(f32[6,1,32]{2,1,0:T(1,128)S(1)} %get-tuple-element.116), channel_id=1, source_target_pairs={{1,0},{2,1},{3,2},{5,4},{6,5},{7,6},{9,8},{10,9},{11,10},{13,12},{... | collective-permute-start | bytes 2312 | tf_op jit(solution)/shard_map/ppermute | solution.py:43
  180.2 10.3 %collective-permute-start.27 = (f32[6,1,32]{2,1,0:T(1,128)S(1)}, f32[6,1,32]{2,1,0:T(1,128)S(1)}, u32[]{:S(2)}, u32[]{:S(2)}) collective-permute-start(f32[6,1,32]{2,1,0:T(1,128)S(1)} %get-tuple-element.115), channel_id=1, source_target_pairs={{0,1},{1,2},{2,3},{4,5},{5,6},{6,7},{8,9},{9,10},{10,11},{12,13},{... | collective-permute-start | bytes 2312 | tf_op jit(solution)/shard_map/ppermute | solution.py:41
  186.2 5.8 %collective-permute-start.20 = (f32[8,1,16,64]{3,2,1,0:T(8,128)S(1)}, f32[8,1,16,64]{3,2,1,0:T(8,128)S(1)}, u32[]{:S(2)}, u32[]{:S(2)}) collective-permute-start(f32[8,1,16,64]{3,2,1,0:T(8,128)S(1)} %get-tuple-element.88), channel_id=1, source_target_pairs={{4,0},{8,4},{12,8},{16,12},{20,16},{24,20},{28,24},{5,1},{9,5},{13... | collective-permute-start | bytes 98312 | tf_op jit(solution)/shard_map/ppermute | solution.py:43
  188.1 5.6 collective-permute-start.21
  193.8 6.7 %collective-permute-start.23 = (f32[8,10,1,64]{3,2,1,0:T(1,128)S(1)}, f32[8,10,1,64]{3,2,1,0:T(1,128)S(1)}, u32[]{:S(2)}, u32[]{:S(2)}) collective-permute-start(f32[8,10,1,64]{3,2,1,0:T(1,128)S(1)} %get-tuple-element.72), channel_id=1, source_target_pairs={{0,1},{1,2},{2,3},{4,5},{5,6},{6,7},{8,9},{9,10},{10,11},{12,13},{... | collective-permute-start | bytes 61448 | tf_op jit(solution)/shard_map/ppermute | solution.py:41
  198.6 5.9 %collective-permute-start.22 = (f32[8,10,1,64]{3,2,1,0:T(1,128)S(1)}, f32[8,10,1,64]{3,2,1,0:T(1,128)S(1)}, u32[]{:S(2)}, u32[]{:S(2)}) collective-permute-start(f32[8,10,1,64]{3,2,1,0:T(1,128)S(1)} %get-tuple-element.71), channel_id=1, source_target_pairs={{1,0},{2,1},{3,2},{5,4},{6,5},{7,6},{9,8},{10,9},{11,10},{13,12},{... | collective-permute-start | bytes 61448 | tf_op jit(solution)/shard_map/ppermute | solution.py:43
  213.7 10.6 %collective-permute-start.28 = (f32[8,1,8,32]{0,3,2,1:T(8,128)S(1)}, f32[8,1,8,32]{0,3,2,1:T(8,128)S(1)}, u32[]{:S(2)}, u32[]{:S(2)}) collective-permute-start(f32[8,1,8,32]{0,3,2,1:T(8,128)S(1)} %get-tuple-element.86), channel_id=1, source_target_pairs={{4,0},{8,4},{12,8},{16,12},{20,16},{24,20},{28,24},{5,1},{9,5},{13... | collective-permute-start | bytes 24584 | tf_op jit(solution)/shard_map/ppermute | solution.py:43
  215.7 8.7 %collective-permute-start.29 = (f32[8,1,8,32]{0,3,2,1:T(8,128)S(1)}, f32[8,1,8,32]{0,3,2,1:T(8,128)S(1)}, u32[]{:S(2)}, u32[]{:S(2)}) collective-permute-start(f32[8,1,8,32]{0,3,2,1:T(8,128)S(1)} %get-tuple-element.85), channel_id=1, source_target_pairs={{0,4},{4,8},{8,12},{12,16},{16,20},{20,24},{24,28},{1,5},{5,9},{9,... | collective-permute-start | bytes 24584 | tf_op jit(solution)/shard_map/ppermute | solution.py:41
  218.8 9.7 %collective-permute-start.37 = (f32[1,4,16]{2,1,0:T(4,128)S(1)}, f32[1,4,16]{2,1,0:T(4,128)S(1)}, u32[]{:S(2)}, u32[]{:S(2)}) collective-permute-start(f32[1,4,16]{2,1,0:T(4,128)S(1)} %get-tuple-element.123), channel_id=1, source_target_pairs={{0,4},{4,8},{8,12},{12,16},{16,20},{20,24},{24,28},{1,5},{5,9},{9,... | collective-permute-start | bytes 776 | tf_op jit(solution)/shard_map/ppermute | solution.py:41
  221.9 6.7 %collective-permute-start.36 = (f32[1,4,16]{2,1,0:T(4,128)S(1)}, f32[1,4,16]{2,1,0:T(4,128)S(1)}, u32[]{:S(2)}, u32[]{:S(2)}) collective-permute-start(f32[1,4,16]{2,1,0:T(4,128)S(1)} %get-tuple-element.122), channel_id=1, source_target_pairs={{4,0},{8,4},{12,8},{16,12},{20,16},{24,20},{28,24},{5,1},{9,5},{13... | collective-permute-start | bytes 776 | tf_op jit(solution)/shard_map/ppermute | solution.py:43
  224.4 10.7 %collective-permute-start.31 = (f32[8,6,1,32]{0,3,2,1:T(8,128)S(1)}, f32[8,6,1,32]{0,3,2,1:T(8,128)S(1)}, u32[]{:S(2)}, u32[]{:S(2)}) collective-permute-start(f32[8,6,1,32]{0,3,2,1:T(8,128)S(1)} %get-tuple-element.66), channel_id=1, source_target_pairs={{0,1},{1,2},{2,3},{4,5},{5,6},{6,7},{8,9},{9,10},{10,11},{12,13},{... | collective-permute-start | bytes 18440 | tf_op jit(solution)/shard_map/ppermute | solution.py:41
  227.2 7.8 %collective-permute-start.30 = (f32[8,6,1,32]{0,3,2,1:T(8,128)S(1)}, f32[8,6,1,32]{0,3,2,1:T(8,128)S(1)}, u32[]{:S(2)}, u32[]{:S(2)}) collective-permute-start(f32[8,6,1,32]{0,3,2,1:T(8,128)S(1)} %get-tuple-element.65), channel_id=1, source_target_pairs={{1,0},{2,1},{3,2},{5,4},{6,5},{7,6},{9,8},{10,9},{11,10},{13,12},{... | collective-permute-start | bytes 18440 | tf_op jit(solution)/shard_map/ppermute | solution.py:43
  228.5 12.5 %collective-permute-start.38 = (f32[4,1,16]{2,1,0:T(1,128)S(1)}, f32[4,1,16]{2,1,0:T(1,128)S(1)}, u32[]{:S(2)}, u32[]{:S(2)}) collective-permute-start(f32[4,1,16]{2,1,0:T(1,128)S(1)} %get-tuple-element.120), channel_id=1, source_target_pairs={{1,0},{2,1},{3,2},{5,4},{6,5},{7,6},{9,8},{10,9},{11,10},{13,12},{... | collective-permute-start | bytes 776 | tf_op jit(solution)/shard_map/ppermute | solution.py:43
  229.8 11.2 %collective-permute-start.39 = (f32[4,1,16]{2,1,0:T(1,128)S(1)}, f32[4,1,16]{2,1,0:T(1,128)S(1)}, u32[]{:S(2)}, u32[]{:S(2)}) collective-permute-start(f32[4,1,16]{2,1,0:T(1,128)S(1)} %get-tuple-element.119), channel_id=1, source_target_pairs={{0,1},{1,2},{2,3},{4,5},{5,6},{6,7},{8,9},{9,10},{10,11},{12,13},{... | collective-permute-start | bytes 776 | tf_op jit(solution)/shard_map/ppermute | solution.py:41
  236.7 5.7 %collective-permute-start.32 = (f32[8,1,8,32]{0,3,2,1:T(8,128)S(1)}, f32[8,1,8,32]{0,3,2,1:T(8,128)S(1)}, u32[]{:S(2)}, u32[]{:S(2)}) collective-permute-start(f32[8,1,8,32]{0,3,2,1:T(8,128)S(1)} %get-tuple-element.84), channel_id=1, source_target_pairs={{4,0},{8,4},{12,8},{16,12},{20,16},{24,20},{28,24},{5,1},{9,5},{13... | collective-permute-start | bytes 24584 | tf_op jit(solution)/shard_map/ppermute | solution.py:43
  238.6 6.3 %collective-permute-start.33 = (f32[8,1,8,32]{0,3,2,1:T(8,128)S(1)}, f32[8,1,8,32]{0,3,2,1:T(8,128)S(1)}, u32[]{:S(2)}, u32[]{:S(2)}) collective-permute-start(f32[8,1,8,32]{0,3,2,1:T(8,128)S(1)} %get-tuple-element.83), channel_id=1, source_target_pairs={{0,4},{4,8},{8,12},{12,16},{16,20},{20,24},{24,28},{1,5},{5,9},{9,... | collective-permute-start | bytes 24584 | tf_op jit(solution)/shard_map/ppermute | solution.py:41
  244.9 7.0 %collective-permute-start.35 = (f32[8,6,1,32]{0,3,2,1:T(8,128)S(1)}, f32[8,6,1,32]{0,3,2,1:T(8,128)S(1)}, u32[]{:S(2)}, u32[]{:S(2)}) collective-permute-start(f32[8,6,1,32]{0,3,2,1:T(8,128)S(1)} %get-tuple-element.64), channel_id=1, source_target_pairs={{0,1},{1,2},{2,3},{4,5},{5,6},{6,7},{8,9},{9,10},{10,11},{12,13},{... | collective-permute-start | bytes 18440 | tf_op jit(solution)/shard_map/ppermute | solution.py:41
  249.8 6.5 %collective-permute-start.34 = (f32[8,6,1,32]{0,3,2,1:T(8,128)S(1)}, f32[8,6,1,32]{0,3,2,1:T(8,128)S(1)}, u32[]{:S(2)}, u32[]{:S(2)}) collective-permute-start(f32[8,6,1,32]{0,3,2,1:T(8,128)S(1)} %get-tuple-element.63), channel_id=1, source_target_pairs={{1,0},{2,1},{3,2},{5,4},{6,5},{7,6},{9,8},{10,9},{11,10},{13,12},{... | collective-permute-start | bytes 18440 | tf_op jit(solution)/shard_map/ppermute | solution.py:43
  263.0 5.4 collective-permute-start.41
  271.3 5.8 %collective-permute-start.42 = (f32[8,4,1,16]{0,3,2,1:T(8,128)S(1)}, f32[8,4,1,16]{0,3,2,1:T(8,128)S(1)}, u32[]{:S(2)}, u32[]{:S(2)}) collective-permute-start(f32[8,4,1,16]{0,3,2,1:T(8,128)S(1)} %get-tuple-element.101), channel_id=1, source_target_pairs={{1,0},{2,1},{3,2},{5,4},{6,5},{7,6},{9,8},{10,9},{11,10},{13,12},{... | collective-permute-start | bytes 6152 | tf_op jit(solution)/shard_map/ppermute | solution.py:43
  281.3 5.6 collective-permute-start.45
  288.3 7.5 %collective-permute-start.47 = (f32[8,4,1,16]{0,3,2,1:T(8,128)}, f32[8,4,1,16]{0,3,2,1:T(8,128)}, u32[]{:S(2)}, u32[]{:S(2)}) collective-permute-start(f32[8,4,1,16]{0,3,2,1:T(8,128)} %get-tuple-element.100), channel_id=1, source_target_pairs={{0,1},{1,2},{2,3},{4,5},{5,6},{6,7},{8,9},{9,10},{10,11},{12,13},{... | collective-permute-start | bytes 6152 | tf_op jit(solution)/shard_map/ppermute | solution.py:41
  291.7 6.1 %collective-permute-start.46 = (f32[8,4,1,16]{0,3,2,1:T(8,128)}, f32[8,4,1,16]{0,3,2,1:T(8,128)}, u32[]{:S(2)}, u32[]{:S(2)}) collective-permute-start(f32[8,4,1,16]{0,3,2,1:T(8,128)} %get-tuple-element.99), channel_id=1, source_target_pairs={{1,0},{2,1},{3,2},{5,4},{6,5},{7,6},{9,8},{10,9},{11,10},{13,12},{... | collective-permute-start | bytes 6152 | tf_op jit(solution)/shard_map/ppermute | solution.py:43
  311.1 23.4 %collective-permute-start.48 = (f32[8,1,8,8]{3,0,2,1:T(8,128)}, f32[8,1,8,8]{3,0,2,1:T(8,128)}, u32[]{:S(2)}, u32[]{:S(2)}) collective-permute-start(f32[8,1,8,8]{3,0,2,1:T(8,128)} %bitcast.10), channel_id=1, source_target_pairs={{0,4},{4,8},{8,12},{12,16},{16,20},{20,24},{24,28},{28,0},{1,5},{5... | collective-permute-start | bytes 6152 | tf_op jit(solution)/shard_map/ppermute | solution.py:20
  355.7 5.1 collective-permute-start.55
  358.9 7.9 %collective-permute-start.56 = (f32[8,1,4,16]{0,3,2,1:T(8,128)S(1)}, f32[8,1,4,16]{0,3,2,1:T(8,128)S(1)}, u32[]{:S(2)}, u32[]{:S(2)}) collective-permute-start(f32[8,1,4,16]{0,3,2,1:T(8,128)S(1)} %get-tuple-element.107), channel_id=1, source_target_pairs={{0,4},{4,8},{8,12},{12,16},{16,20},{20,24},{24,28},{1,5},{5,9},{9,... | collective-permute-start | bytes 6152 | tf_op jit(solution)/shard_map/ppermute | solution.py:41
  370.0 5.8 %collective-permute-start.57 = (f32[8,4,1,16]{0,3,2,1:T(8,128)S(1)}, f32[8,4,1,16]{0,3,2,1:T(8,128)S(1)}, u32[]{:S(2)}, u32[]{:S(2)}) collective-permute-start(f32[8,4,1,16]{0,3,2,1:T(8,128)S(1)} %get-tuple-element.97), channel_id=1, source_target_pairs={{1,0},{2,1},{3,2},{5,4},{6,5},{7,6},{9,8},{10,9},{11,10},{13,12},{... | collective-permute-start | bytes 6152 | tf_op jit(solution)/shard_map/ppermute | solution.py:43
  378.9 5.4 collective-permute-start.60
  384.3 5.9 %collective-permute-start.62 = (f32[8,4,1,16]{0,3,2,1:T(8,128)S(1)}, f32[8,4,1,16]{0,3,2,1:T(8,128)S(1)}, u32[]{:S(2)}, u32[]{:S(2)}) collective-permute-start(f32[8,4,1,16]{0,3,2,1:T(8,128)S(1)} %get-tuple-element.96), channel_id=1, source_target_pairs={{0,1},{1,2},{2,3},{4,5},{5,6},{6,7},{8,9},{9,10},{10,11},{12,13},{... | collective-permute-start | bytes 6152 | tf_op jit(solution)/shard_map/ppermute | solution.py:41
  388.6 5.8 %collective-permute-start.61 = (f32[8,4,1,16]{0,3,2,1:T(8,128)S(1)}, f32[8,4,1,16]{0,3,2,1:T(8,128)S(1)}, u32[]{:S(2)}, u32[]{:S(2)}) collective-permute-start(f32[8,4,1,16]{0,3,2,1:T(8,128)S(1)} %get-tuple-element.95), channel_id=1, source_target_pairs={{1,0},{2,1},{3,2},{5,4},{6,5},{7,6},{9,8},{10,9},{11,10},{13,12},{... | collective-permute-start | bytes 6152 | tf_op jit(solution)/shard_map/ppermute | solution.py:43
  397.8 6.3 %collective-permute-start.64 = (f32[8,1,8,32]{0,3,2,1:T(8,128)S(1)}, f32[8,1,8,32]{0,3,2,1:T(8,128)S(1)}, u32[]{:S(2)}, u32[]{:S(2)}) collective-permute-start(f32[8,1,8,32]{0,3,2,1:T(8,128)S(1)} %get-tuple-element.81), channel_id=1, source_target_pairs={{0,4},{4,8},{8,12},{12,16},{16,20},{20,24},{24,28},{1,5},{5,9},{9,... | collective-permute-start | bytes 24584 | tf_op jit(solution)/shard_map/ppermute | solution.py:41
  406.9 6.5 %collective-permute-start.65 = (f32[8,6,1,32]{0,3,2,1:T(8,128)S(1)}, f32[8,6,1,32]{0,3,2,1:T(8,128)S(1)}, u32[]{:S(2)}, u32[]{:S(2)}) collective-permute-start(f32[8,6,1,32]{0,3,2,1:T(8,128)S(1)} %get-tuple-element.61), channel_id=1, source_target_pairs={{1,0},{2,1},{3,2},{5,4},{6,5},{7,6},{9,8},{10,9},{11,10},{13,12},{... | collective-permute-start | bytes 18440 | tf_op jit(solution)/shard_map/ppermute | solution.py:43
  416.9 6.3 %collective-permute-start.68 = (f32[8,1,8,32]{0,3,2,1:T(8,128)S(1)}, f32[8,1,8,32]{0,3,2,1:T(8,128)S(1)}, u32[]{:S(2)}, u32[]{:S(2)}) collective-permute-start(f32[8,1,8,32]{0,3,2,1:T(8,128)S(1)} %get-tuple-element.79), channel_id=1, source_target_pairs={{0,4},{4,8},{8,12},{12,16},{16,20},{20,24},{24,28},{1,5},{5,9},{9,... | collective-permute-start | bytes 24584 | tf_op jit(solution)/shard_map/ppermute | solution.py:41
  426.1 6.5 %collective-permute-start.69 = (f32[8,6,1,32]{0,3,2,1:T(8,128)S(1)}, f32[8,6,1,32]{0,3,2,1:T(8,128)S(1)}, u32[]{:S(2)}, u32[]{:S(2)}) collective-permute-start(f32[8,6,1,32]{0,3,2,1:T(8,128)S(1)} %get-tuple-element.59), channel_id=1, source_target_pairs={{1,0},{2,1},{3,2},{5,4},{6,5},{7,6},{9,8},{10,9},{11,10},{13,12},{... | collective-permute-start | bytes 18440 | tf_op jit(solution)/shard_map/ppermute | solution.py:43
  445.0 5.6 collective-permute-start.72
  453.5 5.9 %collective-permute-start.73 = (f32[8,10,1,64]{3,2,1,0:T(1,128)S(1)}, f32[8,10,1,64]{3,2,1,0:T(1,128)S(1)}, u32[]{:S(2)}, u32[]{:S(2)}) collective-permute-start(f32[8,10,1,64]{3,2,1,0:T(1,128)S(1)} %get-tuple-element.69), channel_id=1, source_target_pairs={{1,0},{2,1},{3,2},{5,4},{6,5},{7,6},{9,8},{10,9},{11,10},{13,12},{... | collective-permute-start | bytes 61448 | tf_op jit(solution)/shard_map/ppermute | solution.py:43
  462.0 5.6 collective-permute-start.76
  470.5 5.9 %collective-permute-start.77 = (f32[8,10,1,64]{3,2,1,0:T(1,128)S(1)}, f32[8,10,1,64]{3,2,1,0:T(1,128)S(1)}, u32[]{:S(2)}, u32[]{:S(2)}) collective-permute-start(f32[8,10,1,64]{3,2,1,0:T(1,128)S(1)} %get-tuple-element.67), channel_id=1, source_target_pairs={{1,0},{2,1},{3,2},{5,4},{6,5},{7,6},{9,8},{10,9},{11,10},{13,12},{... | collective-permute-start | bytes 61448 | tf_op jit(solution)/shard_map/ppermute | solution.py:43
  522.3 6.3 %collective-permute-start.80 = (f32[8,1,32,128]{3,2,1,0:T(8,128)S(1)}, f32[8,1,32,128]{3,2,1,0:T(8,128)S(1)}, u32[]{:S(2)}, u32[]{:S(2)}) collective-permute-start(f32[8,1,32,128]{3,2,1,0:T(8,128)S(1)} %get-tuple-element.53), channel_id=1, source_target_pairs={{0,4},{4,8},{8,12},{12,16},{16,20},{20,24},{24,28},{1,5},{5,9},{9,... | collective-permute-start | bytes 393224 | tf_op jit(solution)/shard_map/ppermute | solution.py:41
  531.6 6.2 %collective-permute-start.81 = (f32[8,18,1,128]{3,0,2,1:T(8,128)S(1)}, f32[8,18,1,128]{3,0,2,1:T(8,128)S(1)}, u32[]{:S(2)}, u32[]{:S(2)}) collective-permute-start(f32[8,18,1,128]{3,0,2,1:T(8,128)S(1)} %copy.534), channel_id=1, source_target_pairs={{1,0},{2,1},{3,2},{5,4},{6,5},{7,6},{9,8},{10,9},{11,10},{13,12},{... | collective-permute-start | bytes 221192 | tf_op jit(solution)/shard_map/ppermute | solution.py:43
  543.5 6.3 %collective-permute-start.84 = (f32[8,1,32,128]{3,2,1,0:T(8,128)S(1)}, f32[8,1,32,128]{3,2,1,0:T(8,128)S(1)}, u32[]{:S(2)}, u32[]{:S(2)}) collective-permute-start(f32[8,1,32,128]{3,2,1,0:T(8,128)S(1)} %get-tuple-element.51), channel_id=1, source_target_pairs={{0,4},{4,8},{8,12},{12,16},{16,20},{20,24},{24,28},{1,5},{5,9},{9,... | collective-permute-start | bytes 393224 | tf_op jit(solution)/shard_map/ppermute | solution.py:41
  552.8 6.2 %collective-permute-start.85 = (f32[8,18,1,128]{3,0,2,1:T(8,128)S(1)}, f32[8,18,1,128]{3,0,2,1:T(8,128)S(1)}, u32[]{:S(2)}, u32[]{:S(2)}) collective-permute-start(f32[8,18,1,128]{3,0,2,1:T(8,128)S(1)} %copy.538), channel_id=1, source_target_pairs={{1,0},{2,1},{3,2},{5,4},{6,5},{7,6},{9,8},{10,9},{11,10},{13,12},{... | collective-permute-start | bytes 221192 | tf_op jit(solution)/shard_map/ppermute | solution.py:43
  (98 other events, 1767.5 us)
